TPU v7x, 128 devices: a whole 4x4x4 slice. The times are simulated.
128 devices in a mesh: seq: 16 (over x, y), section: 8 (over z, core).
Axes of the slice: x: 4, y: 4, z: 4, core: 2. Of those that a mesh axis runs over, the one named last changes fastest.
Arguments:
- hidden: bfloat16 [8, 6144, 2560], P('section', 'seq'), may hold values from -6 to 6
- query_norm_gain: float32 [8, 2560], P('section'), may hold values from 0.25 to 1.75
- key_norm_gain: float32 [8, 2560], P('section'), may hold values from 0.25 to 1.75
- text_kv: bfloat16 [8, 16, 2, 512, 2560], P('section', 'seq'), may hold values from -6 to 6
- holder: int32 [8], P('section'), may hold values from 0 to 15
- pattern: int32 [48, 7], replicated, may hold values from 0 to 1, as said below
- grad_out: bfloat16 [8, 6144, 2560], P('section', 'seq'), may hold values from -6 to 6
Outputs:
- attended: bfloat16 [8, 6144, 2560], P('section', 'seq')
- upstream: bfloat16 [8, 6144, 2560], P('section', 'seq')
- text_grad: bfloat16 [8, 2, 512, 2560], P('section')
Inputs may be any that keep to these rules, and one draw needn't show every extreme that they name: pattern[b, 3] = 1 for every block b; entries are 0 or 1.
All inputs are finite; a program needn't handle non-finite values.
Results may differ from a plain program's by a relative error of at most 0.0078.
Values may be sent and summed in bfloat16 or wider, within the bound.
A program may use at most 256 MiB of HBM per device.

v0:
```python
import jax
import jax.numpy as jnp
from jax import lax
from jax.sharding import PartitionSpec as P

HDIM = 128
BLK = 128
eps = 1e-06


def extended(cells, sides, width):
    for axis, dim in sides:
        count = lax.axis_size(axis)
        ends = count - 1
        head = lax.slice_in_dim(cells, 0, width, axis=dim)
        tail = lax.slice_in_dim(cells, cells.shape[dim] - width, cells.shape[dim], axis=dim)
        cells = jnp.concatenate(
            [
                lax.ppermute(tail, axis, [(i, (i + 1) % count) for i in range(ends)]),
                cells,
                lax.ppermute(head, axis, [((i + 1) % count, i) for i in range(ends)]),
            ],
            axis=dim,
        )
    return cells


def from_root(block, axis, owner):
    block = jnp.where(lax.axis_index(axis) == owner, block, jnp.zeros_like(block))
    return lax.psum(block, axis)


def shifted(x, axis, by):
    peers = lax.axis_size(axis)
    pairs = [(i, i + by) for i in range(peers) if 0 <= i + by < peers]
    return lax.ppermute(x, axis, pairs)


def norm_forward(hidden_state, norm_gain):
    hidden_float = hidden_state.astype(jnp.float32)
    inverse_root_norm = lax.rsqrt(
        jnp.mean(hidden_float * hidden_float, axis=-1, keepdims=True) + eps
    )
    normalized_input = hidden_float * inverse_root_norm
    return (
        (normalized_input * norm_gain).astype(jnp.bfloat16),
        normalized_input,
        inverse_root_norm,
    )


def norm_backward(upper_bound, norm_gain, normalized_input, inverse_root_norm):
    scaled_input = upper_bound * norm_gain
    return inverse_root_norm * (
        scaled_input
        - normalized_input * jnp.mean(scaled_input * normalized_input, axis=-1, keepdims=True)
    )


def block_mask(pattern, slab, bpd, nslab):
    span = pattern.shape[1]
    rows = lax.dynamic_slice_in_dim(pattern, slab * bpd, bpd, 0)
    first = jnp.arange(bpd, dtype=jnp.int32)[:, None]
    second = jnp.arange(3 * bpd, dtype=jnp.int32)[None, :]
    offset = second - first
    onehot = offset[:, :, None] == jnp.arange(span, dtype=jnp.int32)[None, None, :]
    picked = jnp.sum(jnp.where(onehot, rows[:, None, :], 0), axis=-1)
    globe = slab * bpd - bpd + second
    inside = (globe >= 0) & (globe < nslab * bpd)
    return (picked > 0) & inside


def token_mask(blocks):
    return jnp.repeat(jnp.repeat(blocks, BLK, axis=0), BLK, axis=1)


def divide_heads(x):
    return x.reshape(x.shape[0], x.shape[1] // HDIM, HDIM).transpose(1, 0, 2)


def join_heads(x):
    return x.transpose(1, 0, 2).reshape(x.shape[1], x.shape[0] * x.shape[2])


def query_side(qh, kh, vh, tkh, tvh, doh, attend_mask):
    scale = qh.shape[-1] ** (-0.5)
    keys = jnp.concatenate([kh, tkh], axis=0)
    vals = jnp.concatenate([vh, tvh], axis=0)
    full = jnp.concatenate([attend_mask, jnp.ones((qh.shape[0], tkh.shape[0]), bool)], axis=1)
    scores = jnp.dot(qh, keys.T, preferred_element_type=jnp.float32) * scale
    scores = jnp.where(full, scores, -1e30)
    top = jnp.max(scores, axis=1, keepdims=True)
    total = jnp.sum(jnp.where(full, jnp.exp(scores - top), 0.0), axis=1, keepdims=True)
    lse = top + jnp.log(total)
    probs = jnp.where(full, jnp.exp(scores - lse), 0.0)
    probs_b = probs.astype(jnp.bfloat16)
    out = jnp.dot(probs_b, vals, preferred_element_type=jnp.float32)
    dprob = jnp.dot(doh, vals.T, preferred_element_type=jnp.float32)
    delta = jnp.sum(doh.astype(jnp.float32) * out, axis=1)
    dscore = (probs * (dprob - delta[:, None]) * scale).astype(jnp.bfloat16)
    query_gradient = jnp.dot(dscore, keys, preferred_element_type=jnp.float32)
    dkeys = jnp.dot(dscore.T, qh, preferred_element_type=jnp.float32)
    dvals = jnp.dot(probs_b.T, doh, preferred_element_type=jnp.float32)
    return (out, lse[:, 0], delta, query_gradient, dkeys, dvals)


def local(hidden, query_norm_gain, key_norm_gain, text_kv, holder, pattern, grad_out):
    hidden_state = hidden[0]
    output_gradient = grad_out[0]
    token_rows = hidden_state.shape[0]
    bpd = token_rows // BLK
    slab = lax.axis_index("seq")
    nslab = lax.axis_size("seq")
    normed_query, normalized_input, inverse_root_norm = norm_forward(
        hidden_state, query_norm_gain[0]
    )
    kn, _, _ = norm_forward(hidden_state, key_norm_gain[0])
    near = extended(jnp.stack([kn, hidden_state]), (("seq", 1),), token_rows)
    text_tokens = from_root(text_kv[0, 0], "seq", holder[0])
    attend_mask = token_mask(block_mask(pattern, slab, bpd, nslab))

    def each_head_value(a):
        return query_side(a[0], a[1], a[2], a[3], a[4], a[5], attend_mask)

    saved_residuals = lax.map(
        each_head_value,
        (
            divide_heads(normed_query),
            divide_heads(near[0]),
            divide_heads(near[1]),
            divide_heads(text_tokens[0]),
            divide_heads(text_tokens[1]),
            divide_heads(output_gradient),
        ),
    )
    out, lse, delta, query_gradient, dkeys, dvals = saved_residuals
    ext_rows = 3 * token_rows
    dtext_part = jnp.stack([join_heads(dkeys[:, ext_rows:]), join_heads(dvals[:, ext_rows:])])
    ext = jnp.stack([join_heads(dkeys[:, :ext_rows]), join_heads(dvals[:, :ext_rows])])
    from_upper = shifted(ext[:, :token_rows].astype(jnp.bfloat16), "seq", -1).astype(jnp.float32)
    from_lower = shifted(ext[:, 2 * token_rows :].astype(jnp.bfloat16), "seq", 1).astype(
        jnp.float32
    )
    own_rows = ext[:, token_rows : 2 * token_rows] + from_upper + from_lower
    text_total = lax.psum(dtext_part, "seq")
    grad_hidden = (
        own_rows[1]
        + norm_backward(
            join_heads(query_gradient), query_norm_gain[0], normalized_input, inverse_root_norm
        )
        + norm_backward(own_rows[0], key_norm_gain[0], normalized_input, inverse_root_norm)
    )
    upstream = shifted(grad_hidden.astype(jnp.bfloat16), "section", -1)
    attended = join_heads(out).astype(jnp.bfloat16)
    return (attended[None], upstream[None], text_total.astype(jnp.bfloat16)[None])


def solution(mesh):
    in_specs = (
        P("section", "seq", None),
        P("section", None),
        P("section", None),
        P("section", "seq", None, None, None),
        P("section"),
        P(),
        P("section", "seq", None),
    )
    out_specs = (
        P("section", "seq", None),
        P("section", "seq", None),
        P("section", None, None, None),
    )
    return jax.shard_map(local, mesh=mesh, in_specs=in_specs, out_specs=out_specs, check_vma=False)
```

profile of v0, /device:TPU:24, one launch (start us, length us, event | category | flops | bytes accessed | tf_op | source)
XLA Modules:
  0.0 923.3 jit_solution(16334344849139469414)
XLA Ops:
  7.2 2.8 copy.43
  12.4 2.3 pad_maximum_fusion.9
  14.7 2.6 collective-permute-start.1
  17.4 5.3 collective-permute-start
  23.4 8.0 copy.45
  31.3 2.7 select_bitcast_fusion
  34.7 4.0 copy.46
  38.7 3.2 fusion.42
  41.9 93.5 %collective-permute-done.1 = bf16[2,384,2560]{1,2,0:T(8,128)(2,1)} collective-permute-done((bf16[2,384,2560]{1,2,0:T(8,128)(2,1)}, bf16[2,384,2560]{1,2,0:T(8,128)(2,1)}, u32[]{:S(2)}, u32[]{:S(2)}) %collective-permute-start.1) | collective-permute-done | bytes 3932192 | tf_op jit(solution)/shard_map/ppermute | solution.py:21
  135.4 3.1 collective-permute-done
  138.5 5.1 pad_maximum_fusion.7
  143.7 4.9 fusion.45
  148.6 26.1 %all-reduce.4.cloned.1.call-done = bf16[2,512,2560]{1,2,0:T(8,128)(2,1)} async-done(((bf16[2,512,2560]{1,2,0:T(8,128)(2,1)}), bf16[2,512,2560]{1,2,0:T(8,128)(2,1)}) %all-reduce.4.cloned.1.call-update) | async-done | bytes 5242896 | tf_op jit(solution)/shard_map/psum | solution.py:30
  174.6 5.2 fusion.46
  179.8 351.3 %while.17 = (s32[]{:T(128)}, bf16[20,384,128]{1,2,0:T(8,128)(2,1)}, f32[20,384,128]{1,2,0:T(8,128)}, f32[20,1664,128]{1,2,0:T(8,128)}, f32[20,1664,128]{1,2,0:T(...) while((s32[]{:T(128)}, bf16[20,384,128]{1,2,0:T(8,128)(2,1)}, ...), condition=%wide.region_7.8_spmd.clone, body=%wide.region_3.7_spmd.clone.sunk | while | flops 996523264 | bytes 28792892 | solution.py:125
  192.6 2.5 fusion.70
  203.8 2.3 bitcast_dynamic-update-slice_fusion.2
  210.1 2.6 fusion.70
  227.7 2.5 fusion.70
  238.8 2.3 bitcast_dynamic-update-slice_fusion.2
  245.2 2.6 fusion.70
  262.8 2.5 fusion.70
  273.9 2.3 bitcast_dynamic-update-slice_fusion.2
  280.3 2.5 fusion.70
  291.4 2.3 bitcast_dynamic-update-slice_fusion.2
  297.8 2.6 fusion.70
  309.0 2.3 bitcast_dynamic-update-slice_fusion.2
  315.4 2.5 fusion.70
  326.6 2.3 bitcast_dynamic-update-slice_fusion.2
  332.9 2.6 fusion.70
  344.1 2.3 bitcast_dynamic-update-slice_fusion.2
  350.5 2.6 fusion.70
  368.1 2.6 fusion.70
  379.5 2.3 bitcast_dynamic-update-slice_fusion.2
  385.8 2.5 fusion.70
  397.0 2.3 bitcast_dynamic-update-slice_fusion.2
  403.4 2.5 fusion.70
  414.5 2.3 bitcast_dynamic-update-slice_fusion.2
  420.9 2.5 fusion.70
  432.0 2.3 bitcast_dynamic-update-slice_fusion.2
  438.4 2.6 fusion.70
  449.6 2.3 bitcast_dynamic-update-slice_fusion.2
  456.0 2.6 fusion.70
  473.6 2.5 fusion.70
  491.2 2.5 fusion.70
  508.7 2.6 fusion.70
  526.3 2.6 fusion.70
  531.1 9.7 %slice.46 = f32[20,1152,128]{1,2,0:T(8,128)} slice(f32[20,1664,128]{1,2,0:T(8,128)} %get-tuple-element.70), slice={[0:20], [0:1152], [0:128]} | slice | bytes 23592960 | tf_op jit(solution)/shard_map/slice | solution.py:139
  540.9 9.7 %slice.45 = f32[20,1152,128]{1,2,0:T(8,128)} slice(f32[20,1664,128]{1,2,0:T(8,128)} %get-tuple-element.69), slice={[0:20], [0:1152], [0:128]} | slice | bytes 23592960 | tf_op jit(solution)/shard_map/slice | solution.py:139
  550.6 9.0 fusion.29
  559.6 3.6 fusion.44
  563.2 2.7 collective-permute-start.2
  565.9 5.4 collective-permute-start.3
  571.3 5.7 slice.53
  577.0 5.6 slice.52
  582.6 10.1 %pad_maximum_fusion.8 = f32[2,512,2560]{1,2,0:T(8,128)} fusion(f32[1,512,2560]{1,2,0:T(8,128)} %bitcast.170, f32[1,512,2560]{1,2,0:T(8,128)} %bitcast.171), kind=kLoop, calls=%fused_computation.47 | loop fusion | flops 2621440 | bytes 20971520 | tf_op jit(solution)/shard_map/stack | solution.py:138
  592.7 3.9 fusion.40
  596.7 57.5 %collective-permute-done.2 = bf16[2,384,2560]{1,2,0:T(8,128)(2,1)} collective-permute-done((bf16[2,384,2560]{1,2,0:T(8,128)(2,1)}, bf16[2,384,2560]{1,2,0:T(8,128)(2,1)}, u32[]{:S(2)}, u32[]{:S(2)}) %collective-permute-start.2) | collective-permute-done | bytes 3932192 | tf_op jit(solution)/shard_map/ppermute | solution.py:36
  655.4 5.0 fusion.32
  662.5 3.0 fusion.36
  666.9 235.2 %all-reduce.5 = bf16[2,512,2560]{1,2,0:T(8,128)(2,1)} all-reduce(f32[2,512,2560]{1,2,0:T(8,128)} %pad_maximum_fusion.8), channel_id=1, replica_groups=mesh['seq'=16,'section'=8] {'seq'}, use_global_device_ids=true, to_apply=%region_10.11 | all-reduce | flops 2621440 | bytes 15728640 | tf_op jit(solution)/shard_map/psum | solution.py:145
  902.2 2.4 copy.60
  904.6 7.9 copy.62
  912.5 4.0 copy.61
  (398 shorter events, 279.3 us)
Async XLA Ops:
  7.2 26.9 %copy-start = (s32[48,7]{0,1:T(8,128)S(1)}, s32[48,7]{0,1:T(8,128)}, u32[]{:S(2)}) copy-start(s32[48,7]{0,1:T(8,128)} %param.14) | copy-start | bytes 4036
  7.2 3.4 copy-start.7
  7.2 167.4 %all-reduce.4.cloned.1.call-start = ((), (), s32[]{:S(2)}) async-start(), calls=%async_computation | async-start | bytes 10485760 | tf_op jit(solution)/shard_map/psum | solution.py:30
  11.1 1.3 copy-start.2
  14.7 120.7 %collective-permute-start.1 = (bf16[2,384,2560]{1,2,0:T(8,128)(2,1)}, bf16[2,384,2560]{1,2,0:T(8,128)(2,1)}, u32[]{:S(2)}, u32[]{:S(2)}) collective-permute-start(bf16[2,384,2560]{1,2,0:T(8,128)(2,1)} %pad_maximum_fusion.9), channel_id=1, source_target_pairs={{8,0},{16,8},{24,16},{32,24},{40,32},{48,40},{56,48},{64,56},{72,6... | collective-permute-start | bytes 11796488 | tf_op jit(solution)/shard_map/ppermute | solution.py:21
  17.4 121.1 %collective-permute-start = (bf16[2,384,2560]{1,2,0:T(8,128)(2,1)}, bf16[2,384,2560]{1,2,0:T(8,128)(2,1)}, u32[]{:S(2)}, u32[]{:S(2)}) collective-permute-start(bf16[2,384,2560]{1,2,0:T(8,128)(2,1)} %pad_maximum_fusion.9), channel_id=1, source_target_pairs={{0,8},{8,16},{16,24},{24,32},{32,40},{40,48},{48,56},{56,64},{64,7... | collective-permute-start | bytes 11796488 | tf_op jit(solution)/shard_map/ppermute | solution.py:19
  34.0 0.7 copy-start.8
  38.7 99.8 %copy-start.3 = (bf16[1,384,2560]{1,2,0:T(8,128)(2,1)S(1)}, bf16[1,384,2560]{1,2,0:T(8,128)(2,1)}, u32[]{:S(2)}) copy-start(bf16[1,384,2560]{1,2,0:T(8,128)(2,1)} %copy-done.2) | copy-start | bytes 5898244
  185.6 3.9 copy-start.5
  203.1 3.9 copy-start.5
  220.7 3.9 copy-start.5
  238.2 3.9 copy-start.5
  255.7 3.9 copy-start.5
  273.3 3.9 copy-start.5
  290.8 3.9 copy-start.5
  308.3 3.9 copy-start.5
  325.9 3.9 copy-start.5
  343.4 3.9 copy-start.5
  361.1 3.9 copy-start.5
  378.8 3.9 copy-start.5
  396.3 3.9 copy-start.5
  413.8 3.9 copy-start.5
  431.4 3.9 copy-start.5
  448.9 3.9 copy-start.5
  466.6 3.9 copy-start.5
  484.1 3.9 copy-start.5
  501.7 3.9 copy-start.5
  519.3 3.9 copy-start.5
  563.2 91.0 %collective-permute-start.2 = (bf16[2,384,2560]{1,2,0:T(8,128)(2,1)}, bf16[2,384,2560]{1,2,0:T(8,128)(2,1)}, u32[]{:S(2)}, u32[]{:S(2)}) collective-permute-start(bf16[2,384,2560]{1,2,0:T(8,128)(2,1)} %get-tuple-element.175), channel_id=1, source_target_pairs={{8,0},{16,8},{24,16},{32,24},{40,32},{48,40},{56,48},{64,56},{72,6... | collective-permute-start | bytes 11796488 | tf_op jit(solution)/shard_map/ppermute | solution.py:36
  565.9 89.4 %collective-permute-start.3 = (bf16[2,384,2560]{1,2,0:T(8,128)(2,1)}, bf16[2,384,2560]{1,2,0:T(8,128)(2,1)}, u32[]{:S(2)}, u32[]{:S(2)}) collective-permute-start(bf16[2,384,2560]{1,2,0:T(8,128)(2,1)} %get-tuple-element.176), channel_id=1, source_target_pairs={{0,8},{8,16},{16,24},{24,32},{32,40},{40,48},{48,56},{56,64},{64,7... | collective-permute-start | bytes 11796488 | tf_op jit(solution)/shard_map/ppermute | solution.py:36
  582.6 72.8 %slice-start = ((s8[11796480]{0:T(1024)(128)(4,1)}), s8[4194304]{0:T(1024)(128)(4,1)S(1)}, s32[]{:S(2)}) async-start(s8[11796480]{0:T(1024)(128)(4,1)} %bitcast.162), calls=%async_computation.1 | async-start | bytes 8388608
  582.6 72.8 %slice-start.1 = ((s8[11796480]{0:T(1024)(128)(4,1)}), s8[4194304]{0:T(1024)(128)(4,1)S(1)}, s32[]{:S(2)}) async-start(s8[11796480]{0:T(1024)(128)(4,1)} %bitcast.162), calls=%async_computation.2 | async-start | bytes 8388608
  582.6 72.8 %slice-start.2 = ((s8[11796480]{0:T(1024)(128)(4,1)}), s8[3407872]{0:T(1024)(128)(4,1)S(1)}, s32[]{:S(2)}) async-start(s8[11796480]{0:T(1024)(128)(4,1)} %bitcast.162), calls=%async_computation.3 | async-start | bytes 6815744
  660.4 2.1 copy-start.4
  665.5 236.7 %copy-start.6 = (bf16[20,384,128]{1,2,0:T(8,128)(2,1)S(1)}, bf16[20,384,128]{1,2,0:T(8,128)(2,1)}, u32[]{:S(2)}) copy-start(bf16[20,384,128]{1,2,0:T(8,128)(2,1)} %get-tuple-element.68) | copy-start | bytes 5898244
  665.5 247.0 %collective-permute-start.4 = (bf16[384,2560]{0,1:T(8,128)(2,1)}, bf16[384,2560]{0,1:T(8,128)(2,1)}, u32[]{:S(2)}, u32[]{:S(2)}) collective-permute-start(bf16[384,2560]{0,1:T(8,128)(2,1)} %fusion.36), channel_id=1, source_target_pairs={{1,0},{2,1},{3,2},{4,3},{5,4},{6,5},{7,6},{9,8},{10,9},{11,10},{12... | collective-permute-start | bytes 5898248 | tf_op jit(solution)/shard_map/ppermute | solution.py:36
  904.6 11.9 %copy-start.1 = (s32[48,7]{0,1:T(8,128)S(1)}, s32[48,7]{0,1:T(8,128)}, u32[]{:S(2)}) copy-start(s32[48,7]{0,1:T(8,128)} %param.14) | copy-start | bytes 4036
Sparse Core Ops, SparseCore 0:
  34.2 140.4 all-reduce.3
where the time goes:
time: 929 us; the launch traced here: 923 us
  matrix products  237 us (26%)
  blocking collectives  235 us (25%)
  waiting for transfers between devices  181 us (19%)
  local copies, waits for them, and re-layouts  158 us (17%)
  other arithmetic  78.9 us (8%)
  starting transfers between devices  17.5 us (2%)
  between operations  14.9 us (2%)
    psum x1, blocking collectives, local(): text_total = lax.psum(dtext_part, 'seq')  235 us
    ppermute x1, waiting for transfers between devices, extended(): lax.ppermute(head, axis, [((i + 1) % count, i) for i in range(ends)])  93.5 us
    dynamic_slice x120, local copies, waits for them, and re-layouts, local(): lax.map(each_head_value, (divide_heads(normed_query), divide_heads(near[0...  68.1 us
    ppermute x3, waiting for transfers between devices, shifted(): return lax.ppermute(x, axis, pairs)  58.7 us
    dot_general x20, matrix products, query_side(): dvals = jnp.dot(probs_b.T, doh, preferred_element_type=jnp.float32)  51.2 us
    dot_general x20, matrix products, query_side(): out = jnp.dot(probs_b, vals, preferred_element_type=jnp.float32)  46 us
    dot_general x20, matrix products, query_side(): dkeys = jnp.dot(dscore.T, qh, preferred_element_type=jnp.float32)  44.5 us
    dot_general x20, matrix products, query_side(): dprob = jnp.dot(doh, vals.T, preferred_element_type=jnp.float32)  38.1 us
  transfers between devices with their start and end apart: 6, of which 5 were waited for; matrix products, arithmetic and copies ran while one was open for 7% of the time, Pallas kernels for 0%

commit v1 on v0

--- a/solution.py
+++ b/solution.py
@@ -142,7 +142,8 @@
         jnp.float32
     )
     own_rows = ext[:, token_rows : 2 * token_rows] + from_upper + from_lower
-    text_total = lax.psum(dtext_part, "seq")
+    terms = lax.all_gather(dtext_part, "seq")
+    text_total = jnp.sum(terms, axis=0)
     grad_hidden = (
         own_rows[1]
         + norm_backward(

time: 929 us -> 1570 us (1.69)
  waiting for transfers between devices: 181 us -> 1010 us
  blocking collectives: 235 us -> 0 us
  other arithmetic: 78.9 us -> 132 us
  matrix products: 237 us -> 218 us
    all_gather x0 -> x1, waiting for transfers between devices: none -> 718 us  [local(): terms = lax.all_gather(dtext_part, 'seq')]
    psum x1 -> x0, blocking collectives: 235 us -> none  [local(): text_total = lax.psum(dtext_part, 'seq')]
    ppermute x3, waiting for transfers between devices: 58.7 us -> 174 us  [shifted(): return lax.ppermute(x, axis, pairs)]
    reduce_sum x0 -> x1, other arithmetic: none -> 54.1 us  [local(): text_total = jnp.sum(terms, axis=0)]
    dot_general x20, matrix products: 46 us -> 27.8 us  [query_side(): out = jnp.dot(probs_b, vals, preferred_element_type=jnp.float32)]
    unnamed x31 -> x40, local copies, waits for them, and re-layouts: 31.5 us -> 38.2 us
  transfers between devices with their start and end apart: 6 -> 7, of which waited for: 5 -> 7; matrix products, arithmetic and copies ran while one was open for 7% -> 6% of each run, Pallas kernels for 0% -> 0%
where the time goes in v1:
time: 1570 us; the launch traced here: 1560 us
  waiting for transfers between devices  1010 us (64%)
  matrix products  218 us (14%)
  local copies, waits for them, and re-layouts  169 us (11%)
  other arithmetic  132 us (8%)
    all_gather x1, waiting for transfers between devices, local(): terms = lax.all_gather(dtext_part, 'seq')  718 us
    ppermute x3, waiting for transfers between devices, shifted(): return lax.ppermute(x, axis, pairs)  174 us
    ppermute x1, waiting for transfers between devices, extended(): lax.ppermute(head, axis, [((i + 1) % count, i) for i in range(ends)])  93.2 us
    dynamic_slice x120, local copies, waits for them, and re-layouts, local(): lax.map(each_head_value, (divide_heads(normed_query), divide_heads(near[0...  55.5 us
    reduce_sum x1, other arithmetic, local(): text_total = jnp.sum(terms, axis=0)  54.1 us
    dot_general x20, matrix products, query_side(): dvals = jnp.dot(probs_b.T, doh, preferred_element_type=jnp.float32)  51.1 us
    dot_general x20, matrix products, query_side(): dkeys = jnp.dot(dscore.T, qh, preferred_element_type=jnp.float32)  44.3 us
    unnamed x40, local copies, waits for them, and re-layouts  38.2 us
  transfers between devices with their start and end apart: 7, of which 7 were waited for; matrix products, arithmetic and copies ran while one was open for 6% of the time, Pallas kernels for 0%

profile of v1, /device:TPU:24, one launch (start us, length us, event | category | flops | bytes accessed | tf_op | source)
XLA Modules:
  0.0 1564.3 jit_solution(17958936751596153889)
XLA Ops:
  7.2 2.8 copy.62
  11.2 2.6 pad_maximum_fusion.9
  13.7 2.6 collective-permute-start.1
  16.4 5.3 collective-permute-start
  21.7 8.0 copy.64
  30.3 2.7 select_bitcast_fusion
  33.8 4.0 copy.65
  38.0 3.2 fusion.42
  41.2 93.2 %collective-permute-done.1 = bf16[2,384,2560]{1,2,0:T(8,128)(2,1)} collective-permute-done((bf16[2,384,2560]{1,2,0:T(8,128)(2,1)}, bf16[2,384,2560]{1,2,0:T(8,128)(2,1)}, u32[]{:S(2)}, u32[]{:S(2)}) %collective-permute-start.1) | collective-permute-done | bytes 3932192 | tf_op jit(solution)/shard_map/ppermute | solution.py:21
  134.4 3.1 collective-permute-done
  137.5 5.1 pad_maximum_fusion.7
  142.7 4.9 fusion.45
  147.5 26.1 %all-reduce.3.cloned.1.call-done = bf16[2,512,2560]{1,2,0:T(8,128)(2,1)} async-done(((bf16[2,512,2560]{1,2,0:T(8,128)(2,1)}), bf16[2,512,2560]{1,2,0:T(8,128)(2,1)}) %all-reduce.3.cloned.1.call-update) | async-done | bytes 5242896 | tf_op jit(solution)/shard_map/psum | solution.py:30
  173.6 5.2 fusion.46
  178.9 319.6 %while.17 = (s32[]{:T(128)}, bf16[20,384,128]{1,2,0:T(8,128)(2,1)}, f32[20,384,128]{1,2,0:T(8,128)}, f32[20,1664,128]{1,2,0:T(8,128)}, f32[20,1664,128]{1,2,0:T(...) while((s32[]{:T(128)}, bf16[20,384,128]{1,2,0:T(8,128)(2,1)}, ...), condition=%wide.region_7.8_spmd.clone, body=%wide.region_3.7_spmd.clone.sunk | while | flops 996523264 | bytes 28268576 | solution.py:125
  192.3 2.6 fusion.70
  206.1 2.2 fusion.69
  208.3 2.6 fusion.70
  224.3 2.5 fusion.70
  240.2 2.5 fusion.70
  253.9 2.2 fusion.69
  256.2 2.5 fusion.70
  270.0 2.2 fusion.69
  272.2 2.6 fusion.70
  288.1 2.5 fusion.70
  301.9 2.2 fusion.69
  304.1 2.6 fusion.70
  320.1 2.5 fusion.70
  333.8 2.2 fusion.69
  336.1 2.6 fusion.70
  352.1 2.6 fusion.70
  365.8 2.2 fusion.69
  368.1 2.6 fusion.70
  384.1 2.6 fusion.70
  400.0 2.6 fusion.70
  416.0 2.6 fusion.70
  429.8 2.2 fusion.69
  432.0 2.6 fusion.70
  445.8 2.2 fusion.69
  448.0 2.6 fusion.70
  461.8 2.2 fusion.69
  464.0 2.6 fusion.70
  480.0 2.6 fusion.70
  496.0 2.5 fusion.70
  498.5 3.3 slice.53
  501.9 3.3 slice.52
  505.2 5.2 pad_maximum_fusion.8
  510.4 11.4 copy.79
  521.9 10.3 slice.45
  532.2 16.1 %slice.46 = f32[20,1152,128]{1,2,0:T(8,128)} slice(f32[20,1664,128]{1,2,0:T(8,128)} %get-tuple-element.70), slice={[0:20], [0:1152], [0:128]} | slice | bytes 23592960 | tf_op jit(solution)/shard_map/slice | solution.py:139
  548.3 17.4 %fusion.29 = bf16[2,1152,2560]{1,2,0:T(8,128)(2,1)} fusion(f32[1,1152,2560]{1,2,0:T(8,128)} %bitcast.166, f32[1,1152,2560]{1,2,0:T(8,128)} %bitcast.162), kind=kLoop, calls=%fused_computation.45 | loop fusion | flops 5898240 | bytes 35389440 | tf_op jit(solution)/shard_map/convert.3
  565.7 6.8 fusion.44
  572.5 3.9 collective-permute-start.3
  576.4 2.3 collective-permute-start.2
  579.4 167.3 %collective-permute-done.3 = bf16[2,384,2560]{1,2,0:T(8,128)(2,1)} collective-permute-done((bf16[2,384,2560]{1,2,0:T(8,128)(2,1)}, bf16[2,384,2560]{1,2,0:T(8,128)(2,1)}, u32[]{:S(2)}, u32[]{:S(2)}) %collective-permute-start.3) | collective-permute-done | bytes 3932192 | tf_op jit(solution)/shard_map/ppermute | solution.py:36
  746.8 5.6 collective-permute-done.2
  752.4 4.0 fusion.32
  758.5 3.0 fusion.36
  762.8 4.0 copy.81
  767.6 2.4 copy.82
  770.0 717.5 %all-gather.3.cloned.1.call-done = f32[32,512,2560]{2,1,0:T(8,128)} async-done(((f32[2,512,2560]{2,1,0:T(8,128)}), f32[32,512,2560]{2,1,0:T(8,128)}) %all-gather.3.cloned.1.call-update) | async-done | bytes 167772176 | tf_op jit(solution)/shard_map/all_gather | solution.py:145
  1487.5 54.1 %reduce_sum.71 = bf16[2,512,2560]{2,1,0:T(8,128)(2,1)} reduce(f32[16,2,512,2560]{3,2,1,0:T(8,128)} %bitcast.30, f32[]{:T(128)} %constant.36.clone.1), dimensions={0}, to_apply=%region_10.11 | reduce | flops 39321600 | bytes 173015040 | tf_op jit(solution)/shard_map/reduce_sum | solution.py:146
  1541.6 7.9 copy.95
  1549.5 7.9 copy.83
  (372 shorter events, 254.5 us)
Async XLA Ops:
  7.2 26.1 %copy-start = (s32[48,7]{0,1:T(8,128)S(1)}, s32[48,7]{0,1:T(8,128)}, u32[]{:S(2)}) copy-start(s32[48,7]{0,1:T(8,128)} %param.14) | copy-start | bytes 4036
  7.2 3.4 copy-start.7
  7.2 166.5 %all-reduce.3.cloned.1.call-start = ((), (), s32[]{:S(2)}) async-start(), calls=%async_computation | async-start | bytes 10485760 | tf_op jit(solution)/shard_map/psum | solution.py:30
  11.1 2.6 copy-start.2
  13.7 120.7 %collective-permute-start.1 = (bf16[2,384,2560]{1,2,0:T(8,128)(2,1)}, bf16[2,384,2560]{1,2,0:T(8,128)(2,1)}, u32[]{:S(2)}, u32[]{:S(2)}) collective-permute-start(bf16[2,384,2560]{1,2,0:T(8,128)(2,1)} %pad_maximum_fusion.9), channel_id=1, source_target_pairs={{8,0},{16,8},{24,16},{32,24},{40,32},{48,40},{56,48},{64,56},{72,6... | collective-permute-start | bytes 11796488 | tf_op jit(solution)/shard_map/ppermute | solution.py:21
  16.4 121.1 %collective-permute-start = (bf16[2,384,2560]{1,2,0:T(8,128)(2,1)}, bf16[2,384,2560]{1,2,0:T(8,128)(2,1)}, u32[]{:S(2)}, u32[]{:S(2)}) collective-permute-start(bf16[2,384,2560]{1,2,0:T(8,128)(2,1)} %pad_maximum_fusion.9), channel_id=1, source_target_pairs={{0,8},{8,16},{16,24},{24,32},{32,40},{40,48},{48,56},{56,64},{64,7... | collective-permute-start | bytes 11796488 | tf_op jit(solution)/shard_map/ppermute | solution.py:19
  33.0 0.7 copy-start.8
  33.1 1454.4 %all-gather.3.cloned.1.call-start = ((), (), s32[]{:S(2)}) async-start(), calls=%async_computation.1 | async-start | bytes 178257920 | tf_op jit(solution)/shard_map/all_gather | solution.py:145
  38.0 99.5 %copy-start.3 = (bf16[1,384,2560]{1,2,0:T(8,128)(2,1)S(1)}, bf16[1,384,2560]{1,2,0:T(8,128)(2,1)}, u32[]{:S(2)}) copy-start(bf16[1,384,2560]{1,2,0:T(8,128)(2,1)} %copy-done.2) | copy-start | bytes 5898244
  548.3 30.5 %copy-start.6 = (f32[384,20,128]{0,2,1:T(8,128)S(1)}, f32[384,20,128]{0,2,1:T(8,128)}, u32[]{:S(2)}) copy-start(f32[384,20,128]{0,2,1:T(8,128)} %get-tuple-element.181) | copy-start | bytes 11796484
  548.3 204.0 %slice-start.3 = ((s8[11796480]{0:T(1024)(128)(4,1)}), s8[4194304]{0:T(1024)(128)(4,1)S(1)}, s32[]{:S(2)}) async-start(s8[11796480]{0:T(1024)(128)(4,1)} %bitcast.167), calls=%async_computation.5 | async-start | bytes 8388608
  548.3 204.0 %slice-start.4 = ((s8[11796480]{0:T(1024)(128)(4,1)}), s8[4194304]{0:T(1024)(128)(4,1)S(1)}, s32[]{:S(2)}) async-start(s8[11796480]{0:T(1024)(128)(4,1)} %bitcast.167), calls=%async_computation.6 | async-start | bytes 8388608
  565.7 13.1 copy-start.4
  565.7 186.7 %slice-start = ((s8[11796480]{0:T(1024)(128)(4,1)}), s8[4194304]{0:T(1024)(128)(4,1)S(1)}, s32[]{:S(2)}) async-start(s8[11796480]{0:T(1024)(128)(4,1)} %bitcast.163), calls=%async_computation.2 | async-start | bytes 8388608
  565.7 186.7 %slice-start.1 = ((s8[11796480]{0:T(1024)(128)(4,1)}), s8[4194304]{0:T(1024)(128)(4,1)S(1)}, s32[]{:S(2)}) async-start(s8[11796480]{0:T(1024)(128)(4,1)} %bitcast.163), calls=%async_computation.3 | async-start | bytes 8388608
  565.7 186.7 %slice-start.5 = ((s8[11796480]{0:T(1024)(128)(4,1)}), s8[3407872]{0:T(1024)(128)(4,1)S(1)}, s32[]{:S(2)}) async-start(s8[11796480]{0:T(1024)(128)(4,1)} %bitcast.167), calls=%async_computation.7 | async-start | bytes 6815744
  572.5 174.2 %collective-permute-start.3 = (bf16[2,384,2560]{1,2,0:T(8,128)(2,1)}, bf16[2,384,2560]{1,2,0:T(8,128)(2,1)}, u32[]{:S(2)}, u32[]{:S(2)}) collective-permute-start(bf16[2,384,2560]{1,2,0:T(8,128)(2,1)} %get-tuple-element.191), channel_id=1, source_target_pairs={{0,8},{8,16},{16,24},{24,32},{32,40},{40,48},{48,56},{56,64},{64,7... | collective-permute-start | bytes 11796488 | tf_op jit(solution)/shard_map/ppermute | solution.py:36
  576.4 175.9 %collective-permute-start.2 = (bf16[2,384,2560]{1,2,0:T(8,128)(2,1)}, bf16[2,384,2560]{1,2,0:T(8,128)(2,1)}, u32[]{:S(2)}, u32[]{:S(2)}) collective-permute-start(bf16[2,384,2560]{1,2,0:T(8,128)(2,1)} %get-tuple-element.190), channel_id=1, source_target_pairs={{8,0},{16,8},{24,16},{32,24},{40,32},{48,40},{56,48},{64,56},{72,6... | collective-permute-start | bytes 11796488 | tf_op jit(solution)/shard_map/ppermute | solution.py:36
  578.8 173.6 %slice-start.2 = ((s8[11796480]{0:T(1024)(128)(4,1)}), s8[3407872]{0:T(1024)(128)(4,1)S(1)}, s32[]{:S(2)}) async-start(s8[11796480]{0:T(1024)(128)(4,1)} %bitcast.163), calls=%async_computation.4 | async-start | bytes 6815744
  756.4 2.1 copy-start.5
  761.5 6.1 collective-permute-start.4
  1549.5 7.9 copy-start.1
Sparse Core Ops, SparseCore 0:
  33.2 140.4 all-reduce.2
  522.0 965.4 all-gather.2
